TPU v7x, 32 devices: a whole 2x2x4 slice. The times are simulated.
32 devices in a mesh: tok: 8 (over z, x), hid: 4 (over y, core).
Axes of the slice: x: 2, y: 2, z: 4, core: 2. Of those that a mesh axis runs over, the one named last changes fastest.
Arguments:
- tokens: bfloat16 [4096, 5376], P('tok', 'hid'), may hold values from -6 to 6
- norm_gain: bfloat16 [1, 5376], P(None, 'hid'), may hold values from 0.099609375 to 1.8984375
- w_query: bfloat16 [5376, 4096], P('tok', 'hid'), may hold values from -2 to 2
- w_key: bfloat16 [5376, 2048], P('tok', 'hid'), may hold values from -1 to 1
- value_matrix: bfloat16 [5376, 2048], P('tok', 'hid'), may hold values from -0.078125 to 0.078125
- q_norm_gain: bfloat16 [1, 128], replicated, may hold values from 0.1 to 8
- k_norm_gain: bfloat16 [1, 128], replicated, may hold values from 0.1 to 8
- w_out: bfloat16 [4096, 5376], P('hid'), may hold values from -0.125 to 0.125
Outputs:
- attended: bfloat16 [4096, 5376], P('tok', 'hid')
All inputs are finite; a program needn't handle non-finite values.
Results may differ from a plain program's by a relative error of at most 0.017.
Values may be sent and summed in bfloat16 or wider, within the bound.
A program may use at most 128 MiB of HBM per device.

v0:
```python
import math

import jax
import jax.numpy as jnp
from jax import lax
from jax.sharding import PartitionSpec as P

HEAD_SIZE = 128
WINDOW = 1024


score_scale = 168.0 ** (-0.5)


def shifted(value, axis, steps):
    count = lax.axis_size(axis)
    leading, last = (max(0, -steps), min(count, count - steps))
    return lax.ppermute(value, axis, [(source, source + steps) for source in range(leading, last)])


def head_norm(field, gain):
    count = field.shape[0]
    heads = field.reshape(count, -1, HEAD_SIZE)
    mean_square = jnp.mean(heads * heads, axis=-1, keepdims=True)
    scaled = (
        heads * lax.rsqrt(mean_square + 1e-06) * gain.astype(jnp.float32).reshape(1, 1, HEAD_SIZE)
    )
    return scaled.reshape(count, -1)


def rotate(field, positions):
    count = field.shape[0]
    heads = field.reshape(count, -1, HEAD_SIZE)
    half = HEAD_SIZE // 2
    inverse = jnp.exp(-math.log(10000.0) * jnp.arange(half, dtype=jnp.float32) * 2.0 / HEAD_SIZE)
    angles = positions.astype(jnp.float32)[:, None] * inverse[None, :]
    cosine = jnp.cos(angles)[:, None, :]
    sine = jnp.sin(angles)[:, None, :]
    first = heads[..., :half]
    second = heads[..., half:]
    turned = jnp.concatenate(
        [first * cosine - second * sine, second * cosine + first * sine], axis=-1
    )
    return turned.reshape(count, -1)


def local(tokens, norm_gain, w_query, w_key, value_matrix, q_norm_gain, k_norm_gain, w_out):
    rows = tokens.shape[0]
    gathered, gain_row = (
        lax.all_gather(tokens, "hid", axis=1, tiled=True),
        lax.all_gather(norm_gain, "hid", axis=1, tiled=True),
    )
    values32 = gathered.astype(jnp.float32)
    scale_rows = lax.rsqrt(jnp.mean(values32 * values32, axis=1, keepdims=True) + 1e-06)
    normed = (values32 * scale_rows * gain_row.astype(jnp.float32)).astype(jnp.bfloat16)
    width_query = w_query.shape[1]
    width_kv = w_key.shape[1]
    pieces = (
        lax.all_gather(w_query, "tok", axis=0, tiled=True),
        lax.all_gather(w_key, "tok", axis=0, tiled=True),
        lax.all_gather(value_matrix, "tok", axis=0, tiled=True),
    )
    query_raw, key_raw, value_raw = tuple(
        (jnp.dot(normed, piece, preferred_element_type=jnp.float32) for piece in pieces)
    )
    tok_index = lax.axis_index("tok")
    positions = tok_index * rows + jnp.arange(rows, dtype=jnp.int32)
    query = rotate(head_norm(query_raw, q_norm_gain), positions).astype(jnp.bfloat16)
    key = rotate(head_norm(key_raw, k_norm_gain), positions).astype(jnp.bfloat16)
    value_rows = value_raw.astype(jnp.bfloat16)
    joined = jnp.concatenate([key, value_rows], axis=1)
    reach = (WINDOW - 1 + rows - 1) // rows
    earlier = []
    moving = joined
    for offset in range(reach):
        moving = shifted(moving, "tok", 1)
        earlier = [moving] + earlier
    window_kv = jnp.concatenate(earlier + [joined], axis=0)
    window_extent = window_kv.shape[0]
    key_pos = (tok_index - reach) * rows + jnp.arange(window_extent, dtype=jnp.int32)
    kv_heads = width_kv // HEAD_SIZE
    query_group_count = width_query // HEAD_SIZE // kv_heads
    query_four_axes = query.reshape(rows, kv_heads, query_group_count, HEAD_SIZE)
    keys_three_axes = window_kv[:, :width_kv].reshape(window_extent, kv_heads, HEAD_SIZE)
    values_three_axes = window_kv[:, width_kv:].reshape(window_extent, kv_heads, HEAD_SIZE)
    scores = (
        jnp.einsum(
            "tkgd,skd->kgts", query_four_axes, keys_three_axes, preferred_element_type=jnp.float32
        )
        * score_scale
    )
    allowed = (
        (key_pos[None, :] <= positions[:, None])
        & (key_pos[None, :] > positions[:, None] - WINDOW)
        & (key_pos[None, :] >= 0)
    )
    masked = jnp.where(allowed, scores, -1e30)
    top = jnp.max(masked, axis=-1, keepdims=True)
    weights = jnp.where(allowed, jnp.exp(masked - top), 0.0)
    total = jnp.sum(weights, axis=-1)
    probs = weights.astype(jnp.bfloat16)
    mixed = jnp.einsum(
        "kgts,skd->tkgd", probs, values_three_axes, preferred_element_type=jnp.float32
    )
    mixed = mixed / jnp.transpose(total, (2, 0, 1))[..., None]
    heads_out = mixed.reshape(rows, width_query).astype(jnp.bfloat16)
    partial_value = jnp.dot(heads_out, w_out, preferred_element_type=jnp.float32)
    return lax.psum_scatter(
        partial_value.astype(jnp.bfloat16), "hid", scatter_dimension=1, tiled=True
    )


def solution(mesh):
    in_specs = (
        P("tok", "hid"),
        P(None, "hid"),
        P("tok", "hid"),
        P("tok", "hid"),
        P("tok", "hid"),
        P(),
        P(),
        P("hid", None),
    )
    out_specs = P("tok", "hid")
    return jax.shard_map(local, mesh=mesh, in_specs=in_specs, out_specs=out_specs, check_vma=False)
```

profile of v0, /device:TPU:29, one launch (start us, length us, event | category | flops | bytes accessed | tf_op | source)
XLA Modules:
  0.0 541.4 jit_solution(11107277001566901028)
XLA Ops:
  6.5 0.7 all-gather.5.cloned.1.call-update
  7.3 0.7 all-gather.7.cloned.1.call-update
  8.1 0.7 all-gather.9.cloned.1.call-update
  8.8 0.5 all-gather.11.cloned.1.call-update
  9.4 1.2 dynamic-slice
  11.3 0.7 reduce
  12.3 10.1 %all-reduce = bf16[5376]{0:T(1024)(128)(2,1)S(1)} all-reduce(bf16[5376]{0:T(1024)(128)(2,1)S(1)} %dynamic-update-slice), channel_id=1, replica_groups=mesh['tok'=8,'hid'=4] {'hid'}, use_global_device_ids=true, to_apply=%add | all-reduce | flops 5376 | bytes 21504
  22.5 1.0 multiply_cosine_fusion
  23.7 27.7 %all-gather.5.cloned.1.call-done = bf16[512,5376]{0,1:T(8,128)(2,1)} async-done(((bf16[512,1344]{0,1:T(8,128)(2,1)}), bf16[512,5376]{0,1:T(8,128)(2,1)}) %all-gather.5.cloned.1.call-update) | async-done | bytes 5505040 | tf_op jit(solution)/shard_map/all_gather | solution.py:50
  51.4 3.8 fusion.7
  55.2 86.7 %all-gather.7.cloned.1.call-done = bf16[5376,512]{1,0:T(8,128)(2,1)} async-done(((bf16[672,512]{1,0:T(8,128)(2,1)}), bf16[5376,512]{1,0:T(8,128)(2,1)}) %all-gather.7.cloned.1.call-update) | async-done | bytes 5505040 | tf_op jit(solution)/shard_map/all_gather | solution.py:60
  141.8 7.6 %multiply_reduce_fusion.1 = (f32[512,4]{0,1:T(4,128)S(1)}, f32[512,512]{0,1:T(8,128)S(1)}) fusion(bf16[5376,512]{1,0:T(8,128)(2,1)} %all-gather.7.cloned.1.call-done, bf16[512,5376]{0,1:T(8,128)(2,1)} %all-gather.5.cloned.1.call-done, f32[5376]{0:T(1024)S(1)} %mul.219, f32[512]{0:T(512)S(1)} %add_rsqrt_fusion.2), kind=kOutput, calls=%fused_computation.29 | convolution fusion | flops 2830104576 | bytes 12090368 | tf_op jit(solution)/shard_map/dot_general | solution.py:64
  149.9 81.8 %all-gather.9.cloned.1.call-done = bf16[5376,512]{1,0:T(8,128)(2,1)} async-done(((bf16[672,512]{1,0:T(8,128)(2,1)}), bf16[5376,512]{1,0:T(8,128)(2,1)}) %all-gather.9.cloned.1.call-update) | async-done | bytes 5505040 | tf_op jit(solution)/shard_map/all_gather | solution.py:61
  231.7 7.6 %convolution_convert_fusion.1 = bf16[512,512]{0,1:T(8,128)(2,1)S(1)} fusion(bf16[5376,512]{1,0:T(8,128)(2,1)} %all-gather.9.cloned.1.call-done, bf16[512,5376]{0,1:T(8,128)(2,1)} %all-gather.5.cloned.1.call-done, f32[5376]{0:T(1024)S(1)} %mul.219, f32[512]{0:T(512)S(1)} %add_rsqrt_fusion.2), kind=kOutput, calls=%fused_computation.25 | convolution fusion | flops 2829844480 | bytes 11557888 | tf_op jit(solution)/shard_map/dot_general | solution.py:64
  239.4 2.2 collective-permute-start
  241.6 67.5 %collective-permute-done = bf16[512,1024]{0,1:T(8,128)(2,1)} collective-permute-done((bf16[512,1024]{0,1:T(8,128)(2,1)S(1)}, bf16[512,1024]{0,1:T(8,128)(2,1)}, u32[]{:S(2)}, u32[]{:S(2)}) %collective-permute-start) | collective-permute-done | bytes 1048608 | tf_op jit(solution)/shard_map/ppermute | solution.py:18
  309.1 2.1 collective-permute-start.1
  311.3 1.9 and_and_fusion
  313.2 20.6 %collective-permute-done.1 = bf16[512,1024]{0,1:T(8,128)(2,1)S(1)} collective-permute-done((bf16[512,1024]{0,1:T(8,128)(2,1)}, bf16[512,1024]{0,1:T(8,128)(2,1)S(1)}, u32[]{:S(2)}, u32[]{:S(2)}) %collective-permute-start.1) | collective-permute-done | bytes 1048608 | tf_op jit(solution)/shard_map/ppermute | solution.py:18
  333.8 10.4 %maximum_maximum_fusion = bf16[1536,1024]{0,1:T(8,128)(2,1)S(1)} fusion(bf16[512,512]{0,1:T(8,128)(2,1)S(1)} %convolution_convert_fusion.1, bf16[512,512]{0,1:T(8,128)(2,1)S(1)} %bitcast.57, bf16[512,1024]{0,1:T(8,128)(2,1)} %collective-permute-done, bf16[512,1024]{0,1:T(8,128)(2,1)S(1)} %collective-permute-done.1), kind=kLoop, calls=%fused_computation.16 | loop fusion | flops 12582912 | bytes 6291456 | tf_op jit(solution)/shard_map/concatenate | solution.py:78
  344.1 1.9 fusion.29
  346.0 80.9 %all-gather.11.cloned.1.call-done = bf16[5376,1024]{1,0:T(8,128)(2,1)} async-done(((bf16[672,1024]{1,0:T(8,128)(2,1)}), bf16[5376,1024]{1,0:T(8,128)(2,1)}) %all-gather.11.cloned.1.call-update) | async-done | bytes 11010064 | tf_op jit(solution)/shard_map/all_gather | solution.py:59
  426.9 11.7 %convolution_bitcast_fusion = f32[64,8,8,128]{3,1,2,0:T(8,128)S(1)} fusion(bf16[5376,1024]{1,0:T(8,128)(2,1)} %all-gather.11.cloned.1.call-done, bf16[512,5376]{0,1:T(8,128)(2,1)} %all-gather.5.cloned.1.call-done, f32[5376]{0:T(1024)S(1)} %mul.219, f32[512]{0:T(512)S(1)} %add_rsqrt_fusion.2), kind=kOutput, calls=%fused_computation.24 | convolution fusion | flops 5648154624 | bytes 18635776 | tf_op jit(solution)/shard_map/dot_general | solution.py:64
  439.1 0.6 multiply_reduce_fusion
  440.0 1.3 multiply_multiply_fusion
  441.3 0.9 subtract_convert_fusion
  442.1 0.6 pad_maximum_fusion.1
  442.7 1.1 copy.24
  443.9 12.1 %fusion.30 = f32[4,2,512]{2,1,0:T(2,128)S(1)} fusion(pred[512,1536]{0,1:T(8,128)(4,1)} %and_and_fusion, bf16[1536,4,128,1]{0,2,3,1:T(8,128)(2,1)S(1)} %bitcast.58, bf16[512,4,2,128]{3,0,2,1:T(8,128)(2,1)} %bitcast.61), kind=kOutput, calls=%fused_computation.54 | convolution fusion | flops 1642071552 | bytes 3424256 | tf_op jit(solution)/shard_map/sub | solution.py:99
  456.0 14.5 %fusion.12 = bf16[512,4,2,128]{0,3,2,1:T(8,128)(2,1)} fusion(bf16[1536,4,128,1]{0,2,3,1:T(8,128)(2,1)S(1)} %bitcast.60, pred[512,1536]{0,1:T(8,128)(4,1)} %and_and_fusion, bf16[1536,4,128,1]{0,2,3,1:T(8,128)(2,1)S(1)} %bitcast.59, bf16[512,4,2,128]{3,0,2,1:T(8,128)(2,1)} %bitcast.62, f32[512,4,2]{0,2,1:T(2,128)S(1)} %bitcast.64), kind=kOutput, calls=%fused_computation.19 | convolution fusion | flops 3253736960 | bytes 6045696 | tf_op jit(solution)/shard_map/kgts,skd->tkgd/dot_general | solution.py:102
  470.5 10.7 %convolution_convert_fusion = bf16[512,5376]{0,1:T(8,128)(2,1)} fusion(bf16[512,1024]{0,1:T(8,128)(2,1)} %bitcast.63, bf16[1024,5376]{1,0:T(8,128)(2,1)} %param.15), kind=kOutput, calls=%fused_computation.14 | convolution fusion | flops 5639897088 | bytes 17563648 | tf_op jit(solution)/shard_map/dot_general | solution.py:107
  481.2 53.4 %reduce-scatter.2.cloned.1.call-done = bf16[512,1344]{0,1:T(8,128)(2,1)} async-done(((bf16[512,5376]{0,1:T(8,128)(2,1)}), bf16[512,1344]{0,1:T(8,128)(2,1)}) %reduce-scatter.2.cloned.1.call-update) | async-done | bytes 1376272 | tf_op jit(solution)/shard_map/reduce_scatter | solution.py:108
  (36 shorter events, 1.9 us)
Async XLA Ops:
  6.5 17.1 %copy-start.2 = (bf16[1,128]{1,0:T(2,128)(2,1)S(1)}, bf16[1,128]{1,0:T(2,128)(2,1)}, u32[]{:S(2)}) copy-start(bf16[1,128]{1,0:T(2,128)(2,1)} %param.14) | copy-start | bytes 772
  6.5 44.9 %all-gather.5.cloned.1.call-start = ((), (), s32[]{:S(2)}) async-start(), calls=%async_computation.1 | async-start | bytes 6881280 | tf_op jit(solution)/shard_map/all_gather | solution.py:50
  7.3 134.6 %all-gather.7.cloned.1.call-start = ((), (), s32[]{:S(2)}) async-start(), calls=%async_computation.2 | async-start | bytes 6193152 | tf_op jit(solution)/shard_map/all_gather | solution.py:60
  8.0 223.7 %all-gather.9.cloned.1.call-start = ((), (), s32[]{:S(2)}) async-start(), calls=%async_computation.3 | async-start | bytes 6193152 | tf_op jit(solution)/shard_map/all_gather | solution.py:61
  8.7 418.2 %all-gather.11.cloned.1.call-start = ((), (), s32[]{:S(2)}) async-start(), calls=%async_computation.4 | async-start | bytes 12386304 | tf_op jit(solution)/shard_map/all_gather | solution.py:59
  9.3 525.3 %reduce-scatter.2.cloned.1.call-start = ((), (), s32[]{:S(2)}) async-start(), calls=%async_computation.5 | async-start | bytes 6881280 | tf_op jit(solution)/shard_map/reduce_scatter | solution.py:108
  149.9 161.4 %copy-start.3 = (bf16[1,128]{1,0:T(2,128)(2,1)S(1)}, bf16[1,128]{1,0:T(2,128)(2,1)}, u32[]{:S(2)}) copy-start(bf16[1,128]{1,0:T(2,128)(2,1)} %param.13) | copy-start | bytes 772
  239.4 69.7 %collective-permute-start = (bf16[512,1024]{0,1:T(8,128)(2,1)S(1)}, bf16[512,1024]{0,1:T(8,128)(2,1)}, u32[]{:S(2)}, u32[]{:S(2)}) collective-permute-start(bf16[512,1024]{0,1:T(8,128)(2,1)S(1)} %pad_maximum_fusion), channel_id=1, source_target_pairs={{0,4},{4,8},{8,12},{12,16},{16,20},{20,24},{24,28},{1,5},{5,9},{9,... | collective-permute-start | bytes 3145736 | tf_op jit(solution)/shard_map/ppermute | solution.py:18
  309.1 24.7 %collective-permute-start.1 = (bf16[512,1024]{0,1:T(8,128)(2,1)}, bf16[512,1024]{0,1:T(8,128)(2,1)S(1)}, u32[]{:S(2)}, u32[]{:S(2)}) collective-permute-start(bf16[512,1024]{0,1:T(8,128)(2,1)} %collective-permute-done), channel_id=1, source_target_pairs={{0,4},{4,8},{8,12},{12,16},{16,20},{20,24},{24,28},{1,5},{5,9},{9,... | collective-permute-start | bytes 3145736 | tf_op jit(solution)/shard_map/ppermute | solution.py:18
  441.3 2.6 copy-start
  443.9 12.1 %copy-start.1 = (bf16[1536,512]{0,1:T(8,128)(2,1)S(1)}, bf16[1536,512]{0,1:T(8,128)(2,1)}, u32[]{:S(2)}) copy-start(bf16[1536,512]{0,1:T(8,128)(2,1)} %get-tuple-element.6) | copy-start | bytes 4718596
Sparse Core Ops, SparseCore 0:
  8.9 42.4 all-gather.4
  53.6 88.2 all-gather.6
  144.0 87.6 all-gather.8
  233.7 193.1 all-gather.10
  481.3 53.2 reduce-scatter.1
where the time goes:
time: 552 us; the launch traced here: 541 us
  waiting for transfers between devices  421 us (76%)
  matrix products  64.2 us (12%)
  other arithmetic  21.6 us (4%)
  between operations  14.3 us (3%)
  blocking collectives  10.1 us (2%)
    ppermute x2, waiting for transfers between devices, shifted(): lax.ppermute(value, axis, [(source, source + steps) for source in range(l...  88.1 us
    all_gather x1, waiting for transfers between devices, local(): lax.all_gather(w_key, 'tok', axis=0, tiled=True)  86.7 us
    all_gather x1, waiting for transfers between devices, local(): lax.all_gather(value_matrix, 'tok', axis=0, tiled=True)  81.8 us
    all_gather x1, waiting for transfers between devices, local(): lax.all_gather(w_query, 'tok', axis=0, tiled=True)  80.9 us
    reduce_scatter x1, waiting for transfers between devices, local(): lax.psum_scatter(partial_value.astype(jnp.bfloat16), 'hid', scatter_dimen...  53.4 us
    all_gather x1, waiting for transfers between devices, local(): lax.all_gather(tokens, 'hid', axis=1, tiled=True)  27.7 us
    dot_general x3, matrix products, local(): jnp.dot(normed, piece, preferred_element_type=jnp.float32)  26.9 us
    dot_general x1, matrix products, local(): jnp.einsum('kgts,skd->tkgd', probs, values_three_axes, preferred_element_...  14.5 us
  transfers between devices with their start and end apart: 7, of which 7 were waited for; matrix products, arithmetic and copies ran while one was open for 7% of the time, Pallas kernels for 0%

commit v1 on v0

v1 whole, which is shorter than its diff:
```python
import functools
import math

import jax
import jax.numpy as jnp
from jax import lax
from jax.experimental import pallas as pl
from jax.experimental.pallas import tpu as pltpu
from jax.sharding import PartitionSpec as P

HEAD = 128
WINDOW = 1024
SCALE = 168.0 ** (-0.5)
GAIN_ROWS = 16
MESH = pl.DeviceIdType.MESH
F32 = jnp.float32
BF16 = jnp.bfloat16


def tok_of(pos, n):
    pos = lax.rem(pos + 2 * n, n)
    return jnp.where(pos < n // 2, 2 * pos, 2 * (n - 1 - pos) + 1)


def project(n, nh, reach, x_ref, wq, wk, wv, qg, kg, cos_ref, sin_ref, q_out, win_out,
            w, xs, normed, acc, win, own_sem, x_send, x_recv, send_sem, recv_sem,
            halo_send, halo_recv):
    t = lax.axis_index("tok")
    h = lax.axis_index("hid")
    half = n // 2
    rows = q_out.shape[1]
    sub = x_ref.shape[0]
    part_heads = w.shape[3] // HEAD
    pos = jnp.where(lax.rem(t, 2) == 0, t // 2, n - 1 - t // 2)
    nxt = (tok_of(pos + 1, n), tok_of(pos - 1, n))

    barrier = pltpu.get_barrier_semaphore()
    near = list(nxt) + [lax.rem(t + d + n, n) for d in (1, -1, 2, -2)]
    for peer in near:
        pl.semaphore_signal(barrier, inc=1, device_id={"tok": peer}, device_id_type=MESH)
    for d in range(1, nh):
        pl.semaphore_signal(
            barrier, inc=1, device_id={"hid": lax.rem(h + d, nh)}, device_id_type=MESH)

    cols = w.shape[3]
    own = [
        pltpu.make_async_copy(src, w.at[t, p], own_sem.at[p])
        for p, src in enumerate((wk, wv, wq.at[:, pl.ds(0, cols)], wq.at[:, pl.ds(cols, cols)]))
    ]
    for copy in own:
        copy.start()
    own_x = pltpu.make_async_copy(x_ref, xs.at[h], own_sem.at[4])
    own_x.start()
    pl.semaphore_wait(barrier, len(near) + nh - 1)

    def hop(way, step, part):
        origin = tok_of(pos - step if way == 0 else pos + step, n)
        return pltpu.make_async_remote_copy(
            src_ref=w.at[origin, part], dst_ref=w.at[origin, part],
            send_sem=send_sem.at[way, step, part], recv_sem=recv_sem.at[way, step, part],
            device_id={"tok": nxt[way]}, device_id_type=MESH)

    def arrival(way, step, part):
        origin = tok_of(pos - step - 1 if way == 0 else pos + step + 1, n)
        return pltpu.make_async_remote_copy(
            src_ref=w.at[origin, part], dst_ref=w.at[origin, part],
            send_sem=send_sem.at[way, step, part], recv_sem=recv_sem.at[way, step, part],
            device_id={"tok": nxt[way]}, device_id_type=MESH)

    def carried(way, step, part):
        return step < half - 1 or part % 2 == way

    def launch(step, parts):
        for part in parts:
            for way in (0, 1):
                if carried(way, step, part):
                    if step == 0:
                        if way == 0:
                            own[part].wait()
                    else:
                        arrival(way, step - 1, part).wait_recv()
                    hop(way, step, part).start()

    def x_copy(d, slot):
        return pltpu.make_async_remote_copy(
            src_ref=x_ref, dst_ref=xs.at[slot], send_sem=x_send.at[d - 1],
            recv_sem=x_recv.at[d - 1],
            device_id={"hid": lax.rem(h + d, nh)}, device_id_type=MESH)

    kv, qq = (0, 1), (2, 3)
    launch(0, kv)
    for d in range(1, nh):
        x_copy(d, h).start()
    for step in range(1, half):
        launch(step, kv)
    launch(0, qq)

    own_x.wait()
    for d in range(1, nh):
        x_copy(d, lax.rem(h - d + nh, nh)).wait_recv()
    block = 128

    def norm_rows(i, _):
        at = pl.ds(pl.multiple_of(i * block, block), block)
        square = jnp.zeros((block, 1), F32)
        for b in range(nh):
            for j in range(sub):
                value = xs[b, j, at, :].astype(F32)
                square = square + jnp.sum(value * value, axis=1, keepdims=True)
        scale = lax.rsqrt(square / (nh * sub * x_ref.shape[2]) + 1e-06)
        for b in range(nh):
            for j in range(sub):
                value = xs[b, j, at, :].astype(F32)
                gain = xs[b, j, pl.ds(rows, GAIN_ROWS), :].astype(F32)[0:1]
                normed[b * sub + j, at, :] = (value * scale * gain).astype(BF16)
        return 0

    lax.fori_loop(0, rows // block, norm_rows, 0)

    def accumulate(part, slab):
        acc[part] += jnp.dot(normed[slab], w[slab, part], preferred_element_type=F32)

    def head_turned(part, j, gain):
        def place(i, _):
            at = pl.ds(pl.multiple_of(i * block, block), block)
            value = acc[part, at, j * HEAD:(j + 1) * HEAD]
            mean = jnp.sum(value * value, axis=1, keepdims=True) / HEAD
            value = value * lax.rsqrt(mean + 1e-06) * gain
            turned = value * cos_ref[at, :] + pltpu.roll(value, HEAD // 2, 1) * sin_ref[at, :]
            yield_at = turned.astype(BF16)
            if part == 0:
                at2 = pl.ds(pl.multiple_of(reach * rows + i * block, block), block)
                win[j, at2, :] = yield_at
            else:
                q_out[(part - 2) * part_heads + j, at, :] = yield_at
            return 0

        lax.fori_loop(0, rows // block, place, 0)

    for part in range(4):
        acc[part] = jnp.zeros(acc.shape[1:], F32)
    for way in (0, 1):
        arrival(way, half - 2, 1 - way).wait_recv()
        arrival(way, half - 1, way).wait_recv()

    def kv_slab(i, _):
        accumulate(0, i)
        accumulate(1, i)
        return 0

    lax.fori_loop(0, n, kv_slab, 0)
    k_gain = kg[...].astype(F32)
    q_gain = qg[...].astype(F32)
    for j in range(part_heads):
        head_turned(0, j, k_gain)
        win[part_heads + j, pl.ds(reach * rows, rows), :] = (
            acc[1, :, j * HEAD:(j + 1) * HEAD].astype(BF16))

    even = lax.rem(t, 2) == 0
    mine = win.at[:, pl.ds(2 * rows, rows), :]
    far = win.at[:, pl.ds(0, rows), :]
    mid = win.at[:, pl.ds(rows, rows), :]

    def halo(k, src, dst, peer):
        return pltpu.make_async_remote_copy(
            src_ref=src, dst_ref=dst, send_sem=halo_send.at[k], recv_sem=halo_recv.at[k],
            device_id={"tok": lax.rem(peer + n, n)}, device_id_type=MESH)

    to_far = halo(0, mine, far, t + 2)
    to_mid = halo(1, mine, mid, t + 1)
    relay = halo(1, far, mid, t - 1)
    has_far = t >= 2
    has_mid = t >= 1
    gives_far = t + 2 < n
    relays = jnp.logical_and(jnp.logical_not(even), has_far)

    @pl.when(gives_far)
    def _():
        to_far.start()

    @pl.when(even)
    def _():
        to_mid.start()

    @pl.when(jnp.logical_not(has_far))
    def _():
        win[:, pl.ds(0, rows), :] = jnp.zeros((win.shape[0], rows, HEAD), BF16)

    @pl.when(jnp.logical_not(has_mid))
    def _():
        win[:, pl.ds(rows, rows), :] = jnp.zeros((win.shape[0], rows, HEAD), BF16)

    for step in range(1, half):
        if step == half - 1:
            @pl.when(has_far)
            def _():
                to_far.wait_recv()

            @pl.when(relays)
            def _():
                relay.start()
        launch(step, qq)

    for way in (0, 1):
        arrival(way, half - 2, 3 - way).wait_recv()

    def q_slab(i, _):
        slab = tok_of(pos - (half - 1) + i, n)
        accumulate(2, slab)
        accumulate(3, slab)
        return 0

    lax.fori_loop(0, n - 1, q_slab, 0)
    last = tok_of(pos + half, n)
    for way in (0, 1):
        arrival(way, half - 1, 2 + way).wait_recv()
        accumulate(2 + way, last)
        for j in range(part_heads):
            head_turned(2 + way, j, q_gain)

    @pl.when(has_mid)
    def _():
        to_mid.wait_recv()

    win_out[...] = win[...]

    @pl.when(gives_far)
    def _():
        to_far.wait_send()

    @pl.when(even)
    def _():
        to_mid.wait_send()

    @pl.when(relays)
    def _():
        relay.wait_send()

    for d in range(1, nh):
        x_copy(d, h).wait_send()
    for parts in (kv, qq):
        for step in range(half):
            for part in parts:
                for way in (0, 1):
                    if carried(way, step, part):
                        hop(way, step, part).wait_send()


def attend(nh, reach, q_ref, win_ref, wo_ref, out_ref, heads, part, sib, pair, got,
           sib_send, sib_recv, y_send, y_recv):
    t = lax.axis_index("tok")
    h = lax.axis_index("hid")
    ny = nh // 2
    y, core = h // 2, lax.rem(h, 2)
    q_heads, rows = q_ref.shape[0], q_ref.shape[1]
    kv_heads = win_ref.shape[0] // 2
    group = q_heads // kv_heads
    width = out_ref.shape[1]
    block = rows // 2
    extent = block + WINDOW

    barrier = pltpu.get_barrier_semaphore()
    for d in range(1, nh):
        pl.semaphore_signal(
            barrier, inc=1, device_id={"hid": lax.rem(h + d, nh)}, device_id_type=MESH)

    def attention(r):
        ahead = reach * rows + r * block - WINDOW
        row = lax.broadcasted_iota(jnp.int32, (block, extent), 0)
        col = lax.broadcasted_iota(jnp.int32, (block, extent), 1)
        first = reach * rows - t * rows - ahead
        allowed = (col <= row + WINDOW) & (col > row) & (col >= first)

        def head(i, _):
            k = win_ref[i, pl.ds(ahead, extent), :]
            v = win_ref[kv_heads + i, pl.ds(ahead, extent), :]
            for g in range(group):
                q = q_ref[i * group + g, pl.ds(r * block, block), :]
                s = lax.dot_general(
                    q, k, (((1,), (1,)), ((), ())), preferred_element_type=F32) * SCALE
                s = jnp.where(allowed, s, -1e30)
                top = jnp.max(s, axis=1, keepdims=True)
                weights = jnp.exp(s - top)
                total = jnp.sum(weights, axis=1, keepdims=True)
                mixed = jnp.dot(weights.astype(BF16), v, preferred_element_type=F32) / total
                heads[i * group + g] = mixed.astype(BF16)
            return 0

        lax.fori_loop(0, kv_heads, head, 0)

    def to_sibling(r, k):
        y2 = lax.rem(y + k, ny)
        return pltpu.make_async_remote_copy(
            src_ref=part.at[r, y2 * 2 + 1 - core], dst_ref=sib.at[r, k],
            send_sem=sib_send.at[r, k], recv_sem=sib_recv.at[r, k],
            device_id={"hid": y * 2 + 1 - core}, device_id_type=MESH)

    def across(r, k):
        y2 = lax.rem(y + k, ny)
        return pltpu.make_async_remote_copy(
            src_ref=pair.at[r, k - 1], dst_ref=got.at[r, k - 1],
            send_sem=y_send.at[r, k - 1], recv_sem=y_recv.at[r, k - 1],
            device_id={"hid": y2 * 2 + core}, device_id_type=MESH)

    def out_project(r):
        mixed = jnp.concatenate([heads[i] for i in range(q_heads)], axis=1)
        for b in range(nh):
            start, end = b * width, (b + 1) * width
            a, e = start // 128 * 128, -(-end // 128) * 128
            value = jnp.dot(mixed, wo_ref[:, a:e], preferred_element_type=F32)
            if start > a:
                value = pltpu.roll(value, (e - a) - (start - a), 1)
            part[r, b] = value[:, :width].astype(BF16)

    order = list(range(1, ny)) + [0]

    def pass_on(r):
        for k in range(1, ny):
            to_sibling(r, k).wait_recv()
            y2 = lax.rem(y + k, ny)
            pair[r, k - 1] = (
                part[r, y2 * 2 + core].astype(F32) + sib[r, k].astype(F32)).astype(BF16)
            across(r, k).start()

    def finish(r):
        to_sibling(r, 0).wait_recv()
        value = part[r, h].astype(F32) + sib[r, 0].astype(F32)
        for k in range(1, ny):
            across(r, k).wait_recv()
            value = value + got[r, k - 1].astype(F32)
        out_ref[pl.ds(r * block, block), :] = value.astype(BF16)

    for r in range(2):
        attention(r)
        out_project(r)
        if r == 0:
            pl.semaphore_wait(barrier, nh - 1)
        for k in order:
            to_sibling(r, k).start()
        pass_on(r)
    for r in range(2):
        finish(r)
    for r in range(2):
        for k in order:
            to_sibling(r, k).wait_send()
        for k in range(1, ny):
            across(r, k).wait_send()


def local(n, nh, tokens, norm_gain, w_query, w_key, value_matrix, q_norm_gain, k_norm_gain, w_out):
    rows, feat = tokens.shape
    slab, kv_cols = w_key.shape
    sub = feat // slab
    q_heads, kv_heads = w_query.shape[1] // HEAD, kv_cols // HEAD
    reach = (WINDOW - 1 + rows - 1) // rows
    width = w_out.shape[1] // nh
    half = n // 2
    extended = jnp.concatenate(
        [tokens, jnp.broadcast_to(norm_gain, (GAIN_ROWS, feat))], axis=0)
    extended = jnp.transpose(extended.reshape(rows + GAIN_ROWS, sub, slab), (1, 0, 2))
    inverse = jnp.exp(
        -math.log(10000.0) * jnp.arange(HEAD // 2, dtype=F32) * 2.0 / HEAD)
    positions = lax.axis_index("tok") * rows + jnp.arange(rows, dtype=jnp.int32)
    angles = positions.astype(F32)[:, None] * inverse[None, :]
    cosine, sine = jnp.cos(angles), jnp.sin(angles)
    cosine = jnp.concatenate([cosine, cosine], axis=1)
    sine = jnp.concatenate([-sine, sine], axis=1)

    vmem = pl.BlockSpec(memory_space=pltpu.VMEM)
    hbm = pl.BlockSpec(memory_space=pl.ANY)
    dma = pltpu.SemaphoreType.DMA
    query, window = pl.pallas_call(
        functools.partial(project, n, nh, reach),
        out_shape=(
            jax.ShapeDtypeStruct((q_heads, rows, HEAD), BF16),
            jax.ShapeDtypeStruct((2 * kv_heads, (reach + 1) * rows, HEAD), BF16),
        ),
        in_specs=[hbm] * 4 + [vmem] * 4,
        out_specs=(vmem, vmem),
        scratch_shapes=[
            pltpu.VMEM((n, 4, slab, kv_cols), BF16),
            pltpu.VMEM((nh, sub, rows + GAIN_ROWS, slab), BF16),
            pltpu.VMEM((n, rows, slab), BF16),
            pltpu.VMEM((4, rows, kv_cols), F32),
            pltpu.VMEM((2 * kv_heads, (reach + 1) * rows, HEAD), BF16),
            dma((5,)), dma((nh - 1,)), dma((nh - 1,)),
            dma((2, half, 4)), dma((2, half, 4)), dma((2,)), dma((2,)),
        ],
        compiler_params=pltpu.CompilerParams(
            collective_id=0, has_side_effects=True, vmem_limit_bytes=60 * 2**20),
        name="project",
    )(extended, w_query, w_key, value_matrix, q_norm_gain, k_norm_gain, cosine, sine)

    ny = nh // 2
    block = rows // 2
    return pl.pallas_call(
        functools.partial(attend, nh, reach),
        out_shape=jax.ShapeDtypeStruct((rows, width), BF16),
        in_specs=[vmem] * 3,
        out_specs=vmem,
        scratch_shapes=[
            pltpu.VMEM((q_heads, block, HEAD), BF16),
            pltpu.VMEM((2, nh, block, width), BF16),
            pltpu.VMEM((2, ny, block, width), BF16),
            pltpu.VMEM((2, ny - 1, block, width), BF16),
            pltpu.VMEM((2, ny - 1, block, width), BF16),
            dma((2, ny)), dma((2, ny)), dma((2, ny - 1)), dma((2, ny - 1)),
        ],
        compiler_params=pltpu.CompilerParams(
            collective_id=1, has_side_effects=True, vmem_limit_bytes=56 * 2**20),
        name="attend",
    )(query, window, w_out)


def solution(mesh):
    in_specs = (
        P("tok", "hid"),
        P(None, "hid"),
        P("tok", "hid"),
        P("tok", "hid"),
        P("tok", "hid"),
        P(),
        P(),
        P("hid", None),
    )
    body = functools.partial(local, mesh.shape["tok"], mesh.shape["hid"])
    return jax.shard_map(
        body, mesh=mesh, in_specs=in_specs, out_specs=P("tok", "hid"), check_vma=False)
```

time: 552 us -> 307 us (0.56); the launches traced: 541 us -> 306 us
  waiting for transfers between devices: 421 us -> 0 us
  Pallas kernels: 0 us -> 298 us
  matrix products: 64.2 us -> 0 us
  other arithmetic: 21.6 us -> 2.97 us
  between operations: 14.3 us -> 0.05 us
  blocking collectives: 10.1 us -> 0 us
    pallas_call x0 -> x2, Pallas kernels: none -> 298 us  [the longest x1 244 us: local(): pl.pallas_call(functools.partial(project, n, nh, reach), out_shape=(jax.S...]
    all_gather x4 -> x0, waiting for transfers between devices: 277 us -> none  [the longest x1 86.7 us: local(): lax.all_gather(w_key, 'tok', axis=0, tiled=True)]
    ppermute x2 -> x0, waiting for transfers between devices: 88.1 us -> none  [shifted(): lax.ppermute(value, axis, [(source, source + steps) for source in range(l...]
    reduce_scatter x1 -> x0, waiting for transfers between devices: 53.4 us -> none  [local(): lax.psum_scatter(partial_value.astype(jnp.bfloat16), 'hid', scatter_dimen...]
    dot_general x5 -> x0, matrix products: 52.1 us -> none  [the longest x3 26.9 us: local(): jnp.dot(normed, piece, preferred_element_type=jnp.float32)]
    sub x1 -> x0, matrix products: 12.1 us -> none  [local(): weights = jnp.where(allowed, jnp.exp(masked - top), 0.0)]
    unnamed x1 -> x0, blocking collectives: 10.1 us -> none
    concatenate x4 -> x2, other arithmetic: 11.1 us -> 1.15 us  [the longest x1 1 us: local(): cosine = jnp.concatenate([cosine, cosine], axis=1)]
  transfers between devices with their start and end apart: 7 -> 0, of which waited for: 7 -> 0; matrix products, arithmetic and copies ran while one was open for 7% -> 0% of each run, Pallas kernels for 0% -> 0%
where the time goes in v1:
time: 307 us; the launch traced here: 306 us
  Pallas kernels  298 us (97%)
  local copies, waits for them, and re-layouts  5.14 us (2%)
    pallas_call x1, Pallas kernels, local(): pl.pallas_call(functools.partial(project, n, nh, reach), out_shape=(jax.S...  244 us
    pallas_call x1, Pallas kernels, local(): pl.pallas_call(functools.partial(attend, nh, reach), out_shape=jax.ShapeD...  54 us

profile of v1, /device:TPU:29, one launch (start us, length us, event | category | flops | bytes accessed | tf_op | source)
XLA Modules:
  0.0 306.4 jit_solution(16132971054944266357)
XLA Ops:
  0.0 0.0 copy-start
  0.0 0.8 reduce
  0.8 0.2 broadcast_in_dim.10
  1.1 1.0 fusion
  2.1 1.0 pad_maximum_fusion.1
  3.1 0.0 copy-done
  3.1 0.1 pad_maximum_fusion
  3.2 2.4 copy.11
  5.7 244.2 %project.1 = (bf16[8,512,128]{2,1,0:T(8,128)(2,1)}, bf16[8,1536,128]{2,1,0:T(8,128)(2,1)}) custom-call(bf16[2,528,672]{2,1,0:T(8,128)(2,1)} %bitcast.3, bf16[672,1024]{1,0:T(8,128)(2,1)} %wq.1, bf16[672,512]{1,0:T(8,128)(2,1)} %wk.1, bf16[672,512]{1,0:T(8,128)(2,1)} %wv.1, bf16[1,128]{1,0:T(2,128)(2,1)} %qg.1, bf16[1,128]{1,0:T(2,128)(2,1)} %kg.1, ...), custom_call_target="tpu_custom_call" | custom-call | tf_op jit(solution)/shard_map/project/pallas_call | solution.py:372
  249.9 54.0 %attend.1 = bf16[512,1344]{1,0:T(8,128)(2,1)} custom-call(bf16[8,512,128]{2,1,0:T(8,128)(2,1)} %get-tuple-element.7.q_ref, bf16[8,1536,128]{2,1,0:T(8,128)(2,1)} %get-tuple-element.8.win_ref, bf16[1024,5376]{1,0:T(8,128)(2,1)} %wo_ref.1), custom_call_target="tpu_custom_call" | custom-call | tf_op jit(solution)/shard_map/attend/pallas_call | solution.py:396
  303.9 2.5 copy.12
  (2 shorter events, 0.0 us)
Async XLA Ops:
  0.0 3.1 %copy-start = (bf16[512,1344]{0,1:T(8,128)(2,1)S(1)}, bf16[512,1344]{0,1:T(8,128)(2,1)}, u32[]{:S(2)}) copy-start(bf16[512,1344]{0,1:T(8,128)(2,1)} %param.8) | copy-start | bytes 4128772

commit v2 on v1

--- a/solution.py
+++ b/solution.py
@@ -141,14 +141,18 @@
         acc[part] = jnp.zeros(acc.shape[1:], F32)
     for way in (0, 1):
         arrival(way, half - 2, 1 - way).wait_recv()
+    last = tok_of(pos + half, n)
+
+    def kv_slab(i, _):
+        slab = tok_of(pos - (half - 1) + i, n)
+        accumulate(0, slab)
+        accumulate(1, slab)
+        return 0
+
+    lax.fori_loop(0, n - 1, kv_slab, 0)
+    for way in (0, 1):
         arrival(way, half - 1, way).wait_recv()
-
-    def kv_slab(i, _):
-        accumulate(0, i)
-        accumulate(1, i)
-        return 0
-
-    lax.fori_loop(0, n, kv_slab, 0)
+        accumulate(way, last)
     k_gain = kg[...].astype(F32)
     q_gain = qg[...].astype(F32)
     for j in range(part_heads):
@@ -211,7 +215,6 @@
         return 0
 
     lax.fori_loop(0, n - 1, q_slab, 0)
-    last = tok_of(pos + half, n)
     for way in (0, 1):
         arrival(way, half - 1, 2 + way).wait_recv()
         accumulate(2 + way, last)
@@ -246,8 +249,8 @@
                         hop(way, step, part).wait_send()
 
 
-def attend(nh, reach, q_ref, win_ref, wo_ref, out_ref, heads, part, sib, pair, got,
-           sib_send, sib_recv, y_send, y_recv):
+def attend(nh, reach, q_ref, win_ref, wo_hbm, out_ref, wo_ref, heads, part, sib, pair, got,
+           wo_sem, sib_send, sib_recv, y_send, y_recv):
     t = lax.axis_index("tok")
     h = lax.axis_index("hid")
     ny = nh // 2
@@ -259,6 +262,8 @@
     block = rows // 2
     extent = block + WINDOW
 
+    wo_copy = pltpu.make_async_copy(wo_hbm, wo_ref, wo_sem)
+    wo_copy.start()
     barrier = pltpu.get_barrier_semaphore()
     for d in range(1, nh):
         pl.semaphore_signal(
@@ -277,10 +282,10 @@
             for g in range(group):
                 q = q_ref[i * group + g, pl.ds(r * block, block), :]
                 s = lax.dot_general(
-                    q, k, (((1,), (1,)), ((), ())), preferred_element_type=F32) * SCALE
+                    q, k, (((1,), (1,)), ((), ())), preferred_element_type=F32)
                 s = jnp.where(allowed, s, -1e30)
                 top = jnp.max(s, axis=1, keepdims=True)
-                weights = jnp.exp(s - top)
+                weights = jnp.exp2((s - top) * (SCALE * math.log2(math.e)))
                 total = jnp.sum(weights, axis=1, keepdims=True)
                 mixed = jnp.dot(weights.astype(BF16), v, preferred_element_type=F32) / total
                 heads[i * group + g] = mixed.astype(BF16)
@@ -302,15 +307,21 @@
             send_sem=y_send.at[r, k - 1], recv_sem=y_recv.at[r, k - 1],
             device_id={"hid": y2 * 2 + core}, device_id_type=MESH)
 
-    def out_project(r):
+    def project_block(r, b):
         mixed = jnp.concatenate([heads[i] for i in range(q_heads)], axis=1)
-        for b in range(nh):
-            start, end = b * width, (b + 1) * width
-            a, e = start // 128 * 128, -(-end // 128) * 128
-            value = jnp.dot(mixed, wo_ref[:, a:e], preferred_element_type=F32)
-            if start > a:
-                value = pltpu.roll(value, (e - a) - (start - a), 1)
-            part[r, b] = value[:, :width].astype(BF16)
+        start, end = b * width, (b + 1) * width
+        a, e = start // 128 * 128, -(-end // 128) * 128
+        value = jnp.dot(mixed, wo_ref[:, a:e], preferred_element_type=F32)
+        if start > a:
+            value = pltpu.roll(value, (e - a) - (start - a), 1)
+        part[r, b] = value[:, :width].astype(BF16)
+
+    def out_project(r, k):
+        for y2 in range(ny):
+            @pl.when(lax.rem(y + k, ny) == y2)
+            def _():
+                project_block(r, 2 * y2)
+                project_block(r, 2 * y2 + 1)
 
     order = list(range(1, ny)) + [0]
 
@@ -332,12 +343,14 @@
 
     for r in range(2):
         attention(r)
-        out_project(r)
         if r == 0:
             pl.semaphore_wait(barrier, nh - 1)
+            wo_copy.wait()
         for k in order:
+            if k == 0:
+                pass_on(r)
+            out_project(r, k)
             to_sibling(r, k).start()
-        pass_on(r)
     for r in range(2):
         finish(r)
     for r in range(2):
@@ -396,15 +409,16 @@
     return pl.pallas_call(
         functools.partial(attend, nh, reach),
         out_shape=jax.ShapeDtypeStruct((rows, width), BF16),
-        in_specs=[vmem] * 3,
+        in_specs=[vmem, vmem, hbm],
         out_specs=vmem,
         scratch_shapes=[
+            pltpu.VMEM(w_out.shape, BF16),
             pltpu.VMEM((q_heads, block, HEAD), BF16),
             pltpu.VMEM((2, nh, block, width), BF16),
             pltpu.VMEM((2, ny, block, width), BF16),
             pltpu.VMEM((2, ny - 1, block, width), BF16),
             pltpu.VMEM((2, ny - 1, block, width), BF16),
-            dma((2, ny)), dma((2, ny)), dma((2, ny - 1)), dma((2, ny - 1)),
+            dma(()), dma((2, ny)), dma((2, ny)), dma((2, ny - 1)), dma((2, ny - 1)),
         ],
         compiler_params=pltpu.CompilerParams(
             collective_id=1, has_side_effects=True, vmem_limit_bytes=56 * 2**20),

time: 307 us -> 302 us (0.984)
  Pallas kernels: 298 us -> 294 us
    pallas_call x1, Pallas kernels: 54 us -> 49.4 us  [local(): pl.pallas_call(functools.partial(attend, nh, reach), out_shape=jax.ShapeD...]
where the time goes in v2:
time: 302 us
  Pallas kernels  294 us (97%)
  local copies, waits for them, and re-layouts  5.14 us (2%)
    pallas_call x1, Pallas kernels, local(): pl.pallas_call(functools.partial(project, n, nh, reach), out_shape=(jax.S...  244 us
    pallas_call x1, Pallas kernels, local(): pl.pallas_call(functools.partial(attend, nh, reach), out_shape=jax.ShapeD...  49.4 us

profile of v2, /device:TPU:29, one launch (start us, length us, event | category | flops | bytes accessed | tf_op | source)
XLA Modules:
  0.0 301.8 jit_solution(7200064153235424303)
XLA Ops:
  0.0 0.0 copy-start
  0.0 0.8 reduce
  0.8 0.2 broadcast_in_dim.10
  1.1 1.0 fusion
  2.1 1.0 pad_maximum_fusion.1
  3.1 0.0 copy-done
  3.1 0.1 pad_maximum_fusion
  3.2 2.4 copy.11
  5.7 244.2 %project.1 = (bf16[8,512,128]{2,1,0:T(8,128)(2,1)}, bf16[8,1536,128]{2,1,0:T(8,128)(2,1)}) custom-call(bf16[2,528,672]{2,1,0:T(8,128)(2,1)} %bitcast.3, bf16[672,1024]{1,0:T(8,128)(2,1)} %wq.1, bf16[672,512]{1,0:T(8,128)(2,1)} %wk.1, bf16[672,512]{1,0:T(8,128)(2,1)} %wv.1, bf16[1,128]{1,0:T(2,128)(2,1)} %qg.1, bf16[1,128]{1,0:T(2,128)(2,1)} %kg.1, ...), custom_call_target="tpu_custom_call" | custom-call | tf_op jit(solution)/shard_map/project/pallas_call | solution.py:385
  249.9 49.4 %attend.1 = bf16[512,1344]{1,0:T(8,128)(2,1)} custom-call(bf16[8,512,128]{2,1,0:T(8,128)(2,1)} %get-tuple-element.7.q_ref, bf16[8,1536,128]{2,1,0:T(8,128)(2,1)} %get-tuple-element.8.win_ref, bf16[1024,5376]{1,0:T(8,128)(2,1)} %wo_hbm.1), custom_call_target="tpu_custom_call" | custom-call | tf_op jit(solution)/shard_map/attend/pallas_call | solution.py:409
  299.3 2.5 copy.12
  (2 shorter events, 0.0 us)
Async XLA Ops:
  0.0 3.1 %copy-start = (bf16[512,1344]{0,1:T(8,128)(2,1)S(1)}, bf16[512,1344]{0,1:T(8,128)(2,1)}, u32[]{:S(2)}) copy-start(bf16[512,1344]{0,1:T(8,128)(2,1)} %param.8) | copy-start | bytes 4128772

commit v3 on v2

--- a/solution.py
+++ b/solution.py
@@ -12,6 +12,7 @@
 WINDOW = 1024
 SCALE = 168.0 ** (-0.5)
 GAIN_ROWS = 16
+BLOCKS = 4
 MESH = pl.DeviceIdType.MESH
 F32 = jnp.float32
 BF16 = jnp.bfloat16
@@ -259,7 +260,7 @@
     kv_heads = win_ref.shape[0] // 2
     group = q_heads // kv_heads
     width = out_ref.shape[1]
-    block = rows // 2
+    block = rows // BLOCKS
     extent = block + WINDOW
 
     wo_copy = pltpu.make_async_copy(wo_hbm, wo_ref, wo_sem)
@@ -341,7 +342,7 @@
             value = value + got[r, k - 1].astype(F32)
         out_ref[pl.ds(r * block, block), :] = value.astype(BF16)
 
-    for r in range(2):
+    for r in range(BLOCKS):
         attention(r)
         if r == 0:
             pl.semaphore_wait(barrier, nh - 1)
@@ -351,9 +352,9 @@
                 pass_on(r)
             out_project(r, k)
             to_sibling(r, k).start()
-    for r in range(2):
+    for r in range(BLOCKS):
         finish(r)
-    for r in range(2):
+    for r in range(BLOCKS):
         for k in order:
             to_sibling(r, k).wait_send()
         for k in range(1, ny):
@@ -405,7 +406,7 @@
     )(extended, w_query, w_key, value_matrix, q_norm_gain, k_norm_gain, cosine, sine)
 
     ny = nh // 2
-    block = rows // 2
+    block = rows // BLOCKS
     return pl.pallas_call(
         functools.partial(attend, nh, reach),
         out_shape=jax.ShapeDtypeStruct((rows, width), BF16),
@@ -414,11 +415,11 @@
         scratch_shapes=[
             pltpu.VMEM(w_out.shape, BF16),
             pltpu.VMEM((q_heads, block, HEAD), BF16),
-            pltpu.VMEM((2, nh, block, width), BF16),
-            pltpu.VMEM((2, ny, block, width), BF16),
-            pltpu.VMEM((2, ny - 1, block, width), BF16),
-            pltpu.VMEM((2, ny - 1, block, width), BF16),
-            dma(()), dma((2, ny)), dma((2, ny)), dma((2, ny - 1)), dma((2, ny - 1)),
+            pltpu.VMEM((BLOCKS, nh, block, width), BF16),
+            pltpu.VMEM((BLOCKS, ny, block, width), BF16),
+            pltpu.VMEM((BLOCKS, ny - 1, block, width), BF16),
+            pltpu.VMEM((BLOCKS, ny - 1, block, width), BF16),
+            dma(()), dma((BLOCKS, ny)), dma((BLOCKS, ny)), dma((BLOCKS, ny - 1)), dma((BLOCKS, ny - 1)),
         ],
         compiler_params=pltpu.CompilerParams(
             collective_id=1, has_side_effects=True, vmem_limit_bytes=56 * 2**20),

time: 302 us -> 299 us (0.990)
  Pallas kernels: 294 us -> 290 us
    pallas_call x1, Pallas kernels: 49.4 us -> 45.7 us  [local(): pl.pallas_call(functools.partial(attend, nh, reach), out_shape=jax.ShapeD...]
where the time goes in v3:
time: 299 us; the launch traced here: 298 us
  Pallas kernels  290 us (97%)
  local copies, waits for them, and re-layouts  5.14 us (2%)
    pallas_call x1, Pallas kernels, local(): pl.pallas_call(functools.partial(project, n, nh, reach), out_shape=(jax.S...  244 us
    pallas_call x1, Pallas kernels, local(): pl.pallas_call(functools.partial(attend, nh, reach), out_shape=jax.ShapeD...  45.7 us

profile of v3, /device:TPU:29, one launch (start us, length us, event | category | flops | bytes accessed | tf_op | source)
XLA Modules:
  0.0 298.1 jit_solution(6283695349140405057)
XLA Ops:
  0.0 0.0 copy-start
  0.0 0.8 reduce
  0.8 0.2 broadcast_in_dim.10
  1.1 1.0 fusion
  2.1 1.0 pad_maximum_fusion.1
  3.1 0.0 copy-done
  3.1 0.1 pad_maximum_fusion
  3.2 2.4 copy.11
  5.7 244.2 %project.1 = (bf16[8,512,128]{2,1,0:T(8,128)(2,1)}, bf16[8,1536,128]{2,1,0:T(8,128)(2,1)}) custom-call(bf16[2,528,672]{2,1,0:T(8,128)(2,1)} %bitcast.3, bf16[672,1024]{1,0:T(8,128)(2,1)} %wq.1, bf16[672,512]{1,0:T(8,128)(2,1)} %wk.1, bf16[672,512]{1,0:T(8,128)(2,1)} %wv.1, bf16[1,128]{1,0:T(2,128)(2,1)} %qg.1, bf16[1,128]{1,0:T(2,128)(2,1)} %kg.1, ...), custom_call_target="tpu_custom_call" | custom-call | tf_op jit(solution)/shard_map/project/pallas_call | solution.py:386
  249.9 45.7 %attend.1 = bf16[512,1344]{1,0:T(8,128)(2,1)} custom-call(bf16[8,512,128]{2,1,0:T(8,128)(2,1)} %get-tuple-element.7.q_ref, bf16[8,1536,128]{2,1,0:T(8,128)(2,1)} %get-tuple-element.8.win_ref, bf16[1024,5376]{1,0:T(8,128)(2,1)} %wo_hbm.1), custom_call_target="tpu_custom_call" | custom-call | tf_op jit(solution)/shard_map/attend/pallas_call | solution.py:410
  295.6 2.5 copy.12
  (2 shorter events, 0.0 us)
Async XLA Ops:
  0.0 3.1 %copy-start = (bf16[512,1344]{0,1:T(8,128)(2,1)S(1)}, bf16[512,1344]{0,1:T(8,128)(2,1)}, u32[]{:S(2)}) copy-start(bf16[512,1344]{0,1:T(8,128)(2,1)} %param.8) | copy-start | bytes 4128772
